TPU v7x, 128 devices: a whole 4x4x4 slice. The times are simulated.
128 devices in a mesh: gx: 8 (over y, x_lo), gy: 4 (over x_hi, core), gz: 4 (over z).
Axes of the slice: x: 4 (x_hi: 2, x_lo: 2; x = x_hi * 2 + x_lo), y: 4, z: 4, core: 2. Of those that a mesh axis runs over, the one named last changes fastest.
Arguments:
- latent: float32 [128, 64, 2048], P('gx', 'gy', 'gz'), may hold values from -6 to 6
- conv_first: bfloat16 [3, 3, 192, 64], replicated, may hold values from -0.15625 to 0.15625
- conv_second: bfloat16 [3, 3, 192, 64], replicated, may hold values from -0.15625 to 0.15625
- time_weight: float32 [64, 64], replicated, may hold values from -0.75 to 0.75
- timesteps: int32 [4], replicated, may hold values from 1 to 999
- offsets: int32 [4, 3], replicated, may hold values from 0 to 1, as said below
Outputs:
- denoised: float32 [128, 64, 2048], P('gx', 'gy', 'gz')
Inputs may be any that keep to these rules, and one draw needn't show every extreme that they name: `offsets`: every entry is 0 or 1, and each of the three columns holds at least one 0 and at least one 1.
All inputs are finite; a program needn't handle non-finite values.
Results may differ from a plain program's by a relative error of at most 0.0055.
Values sent between devices are 32-bit elements; how exact they have to be, the bound alone decides.
A program may use at most 64 MiB of HBM per device.

v0:
```python
import itertools
import math

import jax
import jax.numpy as jnp
from jax import lax
from jax.experimental import pallas as pl
from jax.experimental.pallas import tpu as pltpu
from jax.sharding import PartitionSpec as P

MESH = pl.DeviceIdType.MESH
F32 = jnp.float32
BF16 = jnp.bfloat16

XS, YS, TILES = 26, 24, 6


def directions():
    every = [d for d in itertools.product((-1, 0, 1), repeat=3) if d != (0, 0, 0)]
    return sorted(every, key=lambda d: -sum(map(abs, d)))


DIRECTIONS = directions()


def sent(d):
    x = {-1: pl.ds(2, 2), 0: pl.ds(2, 16), 1: pl.ds(16, 2)}[d[0]]
    y = {-1: pl.ds(0, 2), 0: pl.ds(0, 16), 1: pl.ds(14, 2)}[d[1]]
    z = {-1: pl.ds(0, 1), 0: pl.ds(0, 4), 1: pl.ds(3, 1)}[d[2]]
    return z, x, y


def landed(d):
    x = {-1: pl.ds(18, 2), 0: pl.ds(2, 16), 1: pl.ds(0, 2)}[d[0]]
    y = {-1: pl.ds(16, 2), 0: pl.ds(0, 16), 1: pl.ds(22, 2)}[d[1]]
    z = {-1: pl.ds(4, 1), 0: pl.ds(0, 4), 1: pl.ds(5, 1)}[d[2]]
    return z, x, y


def neighbour(d):
    place = []
    for name, by in zip(("gx", "gy", "gz"), d):
        size = lax.axis_size(name)
        place.append(lax.rem(lax.axis_index(name) + by + size, size))
    return tuple(place)


def kernel(
    steps, latent_ref, first_ref, second_ref, bias_ref, delta_ref, offsets_ref, out_ref,
    ext, w1, w1c, w2, taps_in, edge_in, hidden, taps_hid, send_sem, recv_sem, load_sem,
):
    loads = [
        pltpu.make_async_copy(
            latent_ref.at[:, :, pl.ds(128 * tile, 128)],
            ext.at[0, tile, pl.ds(2, 16), pl.ds(0, 16)],
            load_sem.at[tile],
        )
        for tile in range(4)
    ]
    for load in loads:
        load.start()
    barrier = pltpu.get_barrier_semaphore()
    for d in DIRECTIONS:
        pl.semaphore_signal(barrier, inc=1, device_id=neighbour(d), device_id_type=MESH)
    pl.semaphore_wait(barrier, len(DIRECTIONS))
    for load in loads:
        load.wait()

    def copies(step):
        return [
            pltpu.make_async_remote_copy(
                src_ref=ext.at[(step, *sent(d))],
                dst_ref=ext.at[(step, *landed(d))],
                send_sem=send_sem.at[step, i],
                recv_sem=recv_sem.at[step, i],
                device_id=neighbour(d),
                device_id_type=MESH,
            )
            for i, d in enumerate(DIRECTIONS)
        ]

    for copy in copies(0):
        copy.start()

    w1[...] = jnp.zeros_like(w1)
    w1c[...] = jnp.zeros_like(w1c)
    w2[...] = jnp.zeros_like(w2)

    def place_weights(tap, carry):
        one = first_ref[tap]
        two = second_ref[tap]
        for out in range(4):
            rows = pl.ds(out * 64, 192)
            lanes = pl.ds(out * 64, 64)
            w1[0, tap, rows, lanes] = one
            w2[tap, rows, lanes] = two
            if out < 2:
                w1c[tap, rows, lanes] = one
        w1[1, tap, pl.ds(0, 128), pl.ds(0, 64)] = one[:128]
        w1[1, tap, pl.ds(128, 128), pl.ds(64, 64)] = one[64:]
        w1[1, tap, pl.ds(128, 192), pl.ds(128, 64)] = one
        w1[1, tap, pl.ds(192, 192), pl.ds(192, 64)] = one
        return carry

    lax.fori_loop(0, 9, place_weights, 0)

    row16 = lax.broadcasted_iota(jnp.int32, (16, 128), 0)

    def step_body(step, carry):
        for copy in copies(step):
            copy.wait_recv()

        flag_x = offsets_ref[step, 0]
        flag_y = offsets_ref[step, 1]
        flag_z = offsets_ref[step, 2]
        on_x = flag_x.astype(F32)
        on_z = flag_z.astype(F32)
        off_x = 1.0 - on_x
        cut_down = row16 == 8 * flag_y
        cut_up = row16 == 15 - 8 * flag_y

        def three_rows(value):
            down = pltpu.roll(value, 1, 0)[:16]
            up = pltpu.roll(value, YS - 1, 0)[:16]
            return jnp.where(cut_down, 0.0, down), value[:16], jnp.where(cut_up, 0.0, up)

        def input_slot(slot, carry):
            outside = jnp.logical_or(slot < 2, slot >= 18)
            keep = jnp.where(outside, on_x, 1.0)
            to = slot + 2 * (slot >= 10).astype(jnp.int32)
            for tile in range(TILES):
                value = ext[step, tile, slot] * (keep if tile < 4 else keep * on_z)
                for tap, rows in enumerate(three_rows(value)):
                    taps_in[tap, to, :, pl.ds(128 * tile, 128)] = rows.astype(BF16)
            return carry

        lax.fori_loop(0, 20, input_slot, 0)
        for tap in range(3):
            taps_in[tap, 10] = (taps_in[tap, 12].astype(F32) * off_x).astype(BF16)
            taps_in[tap, 11] = (taps_in[tap, 9].astype(F32) * off_x).astype(BF16)

        flat = ext.at[step].reshape(TILES, XS * YS, 128)
        slot24 = lax.broadcasted_iota(jnp.int32, (24, 128), 0)
        for tap_x in range(3):
            entry = slot24 + tap_x
            outside = jnp.logical_or(entry < 2, entry >= 18)
            keep = jnp.where(outside, on_x, 1.0)
            if tap_x == 0:
                keep = jnp.where(slot24 == 9, off_x, keep)
            if tap_x == 2:
                keep = jnp.where(slot24 == 8, off_x, keep)
            keep_halo = keep * on_z
            for tap_y in range(3):
                for tile in range(TILES):
                    parts = []
                    for row in ((22 + tap_y) % 24, 15 + tap_y):
                        value = flat[tile, pl.ds(tap_x * YS + row, 24, stride=YS), :]
                        parts.append(value * (keep if tile < 4 else keep_halo))
                    place = pl.ds(128 * tile, 128)
                    edge_in[3 * tap_x + tap_y, :, place] = jnp.concatenate(parts, axis=0).astype(BF16)

        def inputs_for(tiles):
            columns = []
            for tap_x in range(3):
                for tap_y in range(3):
                    for tile in tiles:
                        lanes = pl.ds(tile * 128, 128)
                        columns.append(jnp.concatenate([
                            taps_in[tap_y, pl.ds(tap_x, 9), :, lanes].reshape(144, 128),
                            taps_in[tap_y, pl.ds(11 + tap_x, 9), :, lanes].reshape(144, 128),
                            edge_in[3 * tap_x + tap_y, :, lanes],
                        ], axis=0))
            return jnp.concatenate(columns, axis=1)

        bias = bias_ref[step]
        flat_hidden = hidden.reshape(5, 24 * YS, 128)
        edge_keep = jnp.where(jnp.logical_or(slot24 < 1, slot24 >= 17), on_x, 1.0)

        def keep_hidden(total, tile, keep_lane):
            value = total + bias
            value = value / (1.0 + jnp.exp(-value))
            if keep_lane is not None:
                value = value * keep_lane
            for slot in range(18):
                part = value[16 * slot : 16 * slot + 16]
                if slot in (0, 17):
                    part = part * on_x
                hidden[tile, slot, pl.ds(0, 16)] = part
            for i, row in enumerate((23, 16)):
                part = value[288 + 24 * i : 312 + 24 * i] * edge_keep
                flat_hidden[tile, pl.ds(row, 24, stride=YS), :] = part

        lane128 = lax.broadcasted_iota(jnp.int32, (1, 128), 1)
        total = jnp.dot(inputs_for((5, 0, 1)), w1[0].reshape(3456, 256), preferred_element_type=F32)
        keep_hidden(total[:, :128], 0, jnp.where(lane128 < 64, on_z, 1.0))
        keep_hidden(total[:, 128:], 1, None)
        total = jnp.dot(inputs_for((1, 2, 3)), w1[flag_z].reshape(3456, 256), preferred_element_type=F32)
        keep_hidden(total[:, :128], 2, None)
        keep_hidden(total[:, 128:], 3, None)
        total = jnp.dot(inputs_for((3, 4)), w1c[...].reshape(2304, 128), preferred_element_type=F32)
        keep_hidden(total, 4, jnp.where(lane128 >= 64, on_z, 1.0))

        low = jnp.where(lane128 < 64, 1.0, 1.0 - on_z)
        high = jnp.where(lane128 >= 64, 1.0, 1.0 - on_z)

        def hidden_slot(slot, carry):
            to = slot + 2 * (slot >= 9).astype(jnp.int32)
            for place, (tile, keep) in enumerate(((0, None), (1, None), (2, low), (2, high), (3, None), (4, None))):
                value = hidden[tile, slot]
                if keep is not None:
                    value = value * keep
                for tap, rows in enumerate(three_rows(value)):
                    taps_hid[tap, to, :, pl.ds(128 * place, 128)] = rows.astype(BF16)
            return carry

        lax.fori_loop(0, 18, hidden_slot, 0)
        for tap in range(3):
            taps_hid[tap, 9] = (taps_hid[tap, 11].astype(F32) * off_x).astype(BF16)
            taps_hid[tap, 10] = (taps_hid[tap, 8].astype(F32) * off_x).astype(BF16)

        def hidden_for(tiles):
            columns = []
            for tap_x in range(3):
                for tap_y in range(3):
                    lanes = pl.ds(tiles * 128, 384)
                    columns.append(jnp.concatenate([
                        taps_hid[tap_y, pl.ds(tap_x, 8), :, lanes].reshape(128, 384),
                        taps_hid[tap_y, pl.ds(10 + tap_x, 8), :, lanes].reshape(128, 384),
                    ], axis=0))
            return jnp.concatenate(columns, axis=1)

        delta = delta_ref[step]
        for half in range(2):
            noise = jnp.dot(hidden_for(3 * half), w2[...].reshape(3456, 256), preferred_element_type=F32)
            for tile in range(2):
                part = noise[:, 128 * tile : 128 * tile + 128].reshape(16, 16, 128)
                before = ext[step, 2 * half + tile, pl.ds(2, 16), pl.ds(0, 16)]
                ext[step + 1, 2 * half + tile, pl.ds(2, 16), pl.ds(0, 16)] = before + delta * part

        @pl.when(step + 1 < steps)
        def _():
            for copy in copies(step + 1):
                copy.start()

        return carry

    lax.fori_loop(0, steps, step_body, 0)

    stores = [
        pltpu.make_async_copy(
            ext.at[steps, tile, pl.ds(2, 16), pl.ds(0, 16)],
            out_ref.at[:, :, pl.ds(128 * tile, 128)],
            load_sem.at[tile],
        )
        for tile in range(4)
    ]
    for store in stores:
        store.start()

    def drain(step, carry):
        for copy in copies(step):
            copy.wait_send()
        return carry

    lax.fori_loop(0, steps, drain, 0)
    for store in stores:
        store.wait()


def time_bias(timesteps, time_weight):
    half_c = time_weight.shape[0] // 2
    freqs = jnp.exp(-math.log(10000.0) * jnp.arange(half_c, dtype=F32) / half_c)
    angles = timesteps.astype(F32)[:, None] * freqs
    emb = jnp.concatenate([jnp.sin(angles), jnp.cos(angles)], axis=1)
    return jnp.dot(emb, time_weight, precision=lax.Precision.HIGHEST)


def shards(latent, conv_first, conv_second, time_weight, timesteps, offsets):
    steps = timesteps.shape[0]
    bias = time_bias(timesteps, time_weight)
    bias = jnp.concatenate([bias, bias], axis=1).reshape(steps, 1, 128)
    later = jnp.concatenate([timesteps[1:], jnp.zeros((1,), jnp.int32)])
    delta = (later - timesteps).astype(F32) / 1000.0
    vmem = pl.BlockSpec(memory_space=pltpu.VMEM)
    smem = pl.BlockSpec(memory_space=pltpu.SMEM)
    anywhere = pl.BlockSpec(memory_space=pl.ANY)
    count = len(DIRECTIONS)

    def body(*refs):
        kernel(steps, *refs)

    return pl.pallas_call(
        body,
        out_shape=jax.ShapeDtypeStruct(latent.shape, latent.dtype),
        in_specs=[anywhere, vmem, vmem, vmem, smem, smem],
        out_specs=anywhere,
        scratch_shapes=[
            pltpu.VMEM((steps + 1, TILES, XS, YS, 128), F32),
            pltpu.VMEM((2, 9, 384, 256), BF16),
            pltpu.VMEM((9, 256, 128), BF16),
            pltpu.VMEM((9, 384, 256), BF16),
            pltpu.VMEM((3, 22, 16, 768), BF16),
            pltpu.VMEM((9, 48, 768), BF16),
            pltpu.VMEM((5, 24, YS, 128), F32),
            pltpu.VMEM((3, 20, 16, 768), BF16),
            pltpu.SemaphoreType.DMA((steps, count)),
            pltpu.SemaphoreType.DMA((steps, count)),
            pltpu.SemaphoreType.DMA((4,)),
        ],
        compiler_params=pltpu.CompilerParams(
            collective_id=0, has_side_effects=True, vmem_limit_bytes=48 * 2**20
        ),
    )(latent, conv_first.reshape(9, 192, 64), conv_second.reshape(9, 192, 64), bias, delta, offsets)


def solution(mesh):
    return jax.shard_map(
        shards,
        mesh=mesh,
        in_specs=(P("gx", "gy", "gz"), P(), P(), P(), P(), P()),
        out_specs=P("gx", "gy", "gz"),
        check_vma=False,
    )
```

profile of v0, /device:TPU:1, one launch (start us, length us, event | category | flops | bytes accessed | tf_op | source)
XLA Modules:
  0.0 68.1 jit_solution(16224383843604352096)
XLA Ops:
  0.0 0.0 copy-start
  0.0 0.0 copy-start.4
  0.0 0.7 %convert_element_type.6 = f32[4]{0:T(128)S(1)} convert(s32[4]{0:T(128)} %param.10) | non-fusion elementwise | flops 4 | bytes 32 | tf_op jit(solution)/shard_map/convert_element_type | solution.py:273
  0.7 0.0 copy-done.4
  0.7 0.1 slice.3
  0.8 0.1 fusion.5.refs_4_
  0.9 0.1 multiply_sine_fusion
  1.0 0.0 copy-done
  1.0 0.2 fusion
  1.2 0.1 pad_maximum_fusion
  1.3 0.0 copy-start.3
  1.3 1.3 %copy.7 = bf16[3,3,192,64]{3,2,1,0:T(8,128)(2,1)S(1)} copy(bf16[3,3,192,64]{2,3,1,0:T(8,128)(2,1)} %param.7) | data formatting | bytes 442368 | tf_op args[1]
  2.6 0.0 copy-start.1
  2.6 0.0 copy-done.3
  2.6 0.0 copy-start.2
  2.6 0.3 copy.8
  2.9 0.8 %copy-done.1 = f32[16,16,512]{2,1,0:T(8,128)S(1)} copy-done((f32[16,16,512]{2,1,0:T(8,128)S(1)}, f32[16,16,512]{2,1,0:T(8,128)}, u32[]{:S(2)}) %copy-start.1) | copy-done | bytes 524312
  3.6 0.0 copy-done.2
  3.6 63.7 %shard_map.64 = f32[16,16,512]{2,1,0:T(8,128)S(1)} custom-call(f32[16,16,512]{2,1,0:T(8,128)S(1)} %copy-done.1, bf16[9,192,64]{2,1,0:T(8,128)(2,1)S(1)} %bitcast.4, bf16[9,192,64]{2,1,0:T(8,128)(2,1)S(1)} %bitcast.5, f32[4,1,128]{2,1,0:T(1,128)S(1)} %bitcast.6, f32[4]{0:T(128)S(1)} %fusion.5.refs_4_, s32[4,3]{1,0:T(4,128)S(1)} %copy-done.2), custom_call_target="tpu_custom_call" | custom-call | tf_op jit(solution)/shard_map/pallas_call | solution.py:292
  67.3 0.8 %copy.10 = f32[16,16,512]{2,1,0:T(8,128)} copy(f32[16,16,512]{2,1,0:T(8,128)S(1)} %shard_map.64) | data formatting | bytes 1048576
  (1 shorter events, 0.0 us)
Async XLA Ops:
  0.0 1.0 %copy-start = (f32[64,64]{1,0:T(8,128)S(1)}, f32[64,64]{1,0:T(8,128)}, u32[]{:S(2)}) copy-start(f32[64,64]{1,0:T(8,128)} %param.9) | copy-start | bytes 49156
  0.0 0.7 %copy-start.4 = (s32[4]{0:T(128)S(1)}, s32[4]{0:T(128)}, u32[]{:S(2)}) copy-start(s32[4]{0:T(128)} %param.10) | copy-start | bytes 52
  1.3 1.3 %copy-start.3 = (bf16[3,3,192,64]{2,3,1,0:T(8,128)(2,1)S(1)}, bf16[3,3,192,64]{2,3,1,0:T(8,128)(2,1)}, u32[]{:S(2)}) copy-start(bf16[3,3,192,64]{2,3,1,0:T(8,128)(2,1)} %param.8) | copy-start | bytes 663556
  2.6 1.1 %copy-start.1 = (f32[16,16,512]{2,1,0:T(8,128)S(1)}, f32[16,16,512]{2,1,0:T(8,128)}, u32[]{:S(2)}) copy-start(f32[16,16,512]{2,1,0:T(8,128)} %refs_0_.1) | copy-start | bytes 1572868
  2.6 1.0 %copy-start.2 = (s32[4,3]{1,0:T(4,128)S(1)}, s32[4,3]{1,0:T(4,128)}, u32[]{:S(2)}) copy-start(s32[4,3]{1,0:T(4,128)} %refs_5_.1) | copy-start | bytes 148
where the time goes:
time: 68.3 us; the launch traced here: 68.1 us
  Pallas kernels  63.7 us (93%)
  local copies, waits for them, and re-layouts  3.18 us (5%)
  other arithmetic  1.01 us (1%)
    pallas_call x1, Pallas kernels, shards(): pl.pallas_call(body, out_shape=jax.ShapeDtypeStruct(latent.shape, latent....  63.7 us
    unnamed x13, local copies, waits for them, and re-layouts  3.11 us

commit v1 on v0

v1 whole, which is shorter than its diff:
```python
import itertools
import math

import jax
import jax.numpy as jnp
from jax import lax
from jax.experimental import pallas as pl
from jax.experimental.pallas import tpu as pltpu
from jax.sharding import PartitionSpec as P

MESH = pl.DeviceIdType.MESH
F32 = jnp.float32
BF16 = jnp.bfloat16

XS, YS, TILES = 20, 24, 6


def directions():
    every = [d for d in itertools.product((-1, 0, 1), repeat=3) if d != (0, 0, 0)]
    return sorted(every, key=lambda d: (d[0] != 0, -sum(map(abs, d))))


DIRECTIONS = directions()


def sent(d):
    x = {-1: pl.ds(2, 2), 0: pl.ds(2, 16), 1: pl.ds(16, 2)}[d[0]]
    y = {-1: pl.ds(0, 2), 0: pl.ds(0, 16), 1: pl.ds(14, 2)}[d[1]]
    z = {-1: pl.ds(0, 1), 0: pl.ds(0, 4), 1: pl.ds(3, 1)}[d[2]]
    return z, x, y


def landed(d):
    x = {-1: pl.ds(18, 2), 0: pl.ds(2, 16), 1: pl.ds(0, 2)}[d[0]]
    y = {-1: pl.ds(16, 2), 0: pl.ds(0, 16), 1: pl.ds(22, 2)}[d[1]]
    z = {-1: pl.ds(4, 1), 0: pl.ds(0, 4), 1: pl.ds(5, 1)}[d[2]]
    return z, x, y


def neighbour(d):
    place = []
    for name, by in zip(("gx", "gy", "gz"), d):
        size = lax.axis_size(name)
        place.append(lax.rem(lax.axis_index(name) + by + size, size))
    return tuple(place)


def kernel(
    steps, latent_ref, first_ref, second_ref, bias_ref, delta_ref, offsets_ref, out_ref,
    ext, w1, w1c, w2, taps_in, edge_in, taps_side, edge_side, partial, hidden, taps_hid, send_sem, recv_sem, load_sem,
):
    loads = [
        pltpu.make_async_copy(
            latent_ref.at[:, :, pl.ds(128 * tile, 128)],
            ext.at[0, tile, pl.ds(2, 16), pl.ds(0, 16)],
            load_sem.at[tile],
        )
        for tile in range(4)
    ]
    for load in loads:
        load.start()
    barrier = pltpu.get_barrier_semaphore()
    for d in DIRECTIONS:
        pl.semaphore_signal(barrier, inc=1, device_id=neighbour(d), device_id_type=MESH)
    pl.semaphore_wait(barrier, len(DIRECTIONS))
    for load in loads:
        load.wait()

    def copies(step, sides=(-1, 0, 1)):
        return [
            pltpu.make_async_remote_copy(
                src_ref=ext.at[(step, *sent(d))],
                dst_ref=ext.at[(step, *landed(d))],
                send_sem=send_sem.at[step, i],
                recv_sem=recv_sem.at[step, i],
                device_id=neighbour(d),
                device_id_type=MESH,
            )
            for i, d in enumerate(DIRECTIONS)
            if d[0] in sides
        ]

    for copy in copies(0):
        copy.start()

    w1[...] = jnp.zeros_like(w1)
    w1c[...] = jnp.zeros_like(w1c)
    w2[...] = jnp.zeros_like(w2)

    def place_weights(tap, carry):
        one = first_ref[tap]
        two = second_ref[tap]
        for out in range(4):
            rows = pl.ds(out * 64, 192)
            lanes = pl.ds(out * 64, 64)
            w1[0, tap, rows, lanes] = one
            w2[tap, rows, lanes] = two
            if out < 2:
                w1c[tap, rows, lanes] = one
        w1[1, tap, pl.ds(0, 128), pl.ds(0, 64)] = one[:128]
        w1[1, tap, pl.ds(128, 128), pl.ds(64, 64)] = one[64:]
        w1[1, tap, pl.ds(128, 192), pl.ds(128, 64)] = one
        w1[1, tap, pl.ds(192, 192), pl.ds(192, 64)] = one
        return carry

    lax.fori_loop(0, 9, place_weights, 0)

    row8 = lax.broadcasted_iota(jnp.int32, (8, 128), 0)
    row16 = lax.broadcasted_iota(jnp.int32, (16, 128), 0)
    lane128 = lax.broadcasted_iota(jnp.int32, (1, 128), 1)
    own_rows = pl.ds(0, 16)

    def step_body(step, carry):
        flag_x = offsets_ref[step, 0]
        flag_y = offsets_ref[step, 1]
        flag_z = offsets_ref[step, 2]
        on_x = flag_x.astype(F32)
        on_y = flag_y.astype(F32)
        on_z = flag_z.astype(F32)
        off_x = 1.0 - on_x
        cut_down = row16 == 8 * flag_y
        cut_up = row16 == 15 - 8 * flag_y
        cut_back = jnp.logical_and(row16 == 8, flag_x == 1)
        cut_ahead = jnp.logical_and(row16 == 7, flag_x == 1)
        bias = bias_ref[step]
        delta = delta_ref[step]
        flat = ext.at[step].reshape(TILES, XS * YS, 128)
        flat_hidden = hidden.reshape(5, 18 * YS, 128)

        def three_rows(value):
            count = value.shape[0]
            down = pltpu.roll(value, 1, 0)[:16]
            up = pltpu.roll(value, count - 1, 0)[:16]
            return jnp.where(cut_down, 0.0, down), value[:16], jnp.where(cut_up, 0.0, up)

        def lanes_of(tile):
            return pl.ds(128 * tile, 128)

        def close_gap(taps, gap, tiles):
            lanes = pl.ds(128 * tiles[0], 128 * len(tiles))
            for tap in range(3):
                taps[tap, gap, :, lanes] = (taps[tap, gap + 2, :, lanes].astype(F32) * off_x).astype(BF16)
                taps[tap, gap + 1, :, lanes] = (taps[tap, gap - 1, :, lanes].astype(F32) * off_x).astype(BF16)

        def input_slots(tiles, keep):
            def one(x, carry):
                to = x + 2 * (x >= 8).astype(jnp.int32)
                for tile in tiles:
                    value = ext[step, tile, x + 2, own_rows]
                    if keep is not None:
                        value = value * keep
                    for tap, rows in enumerate(three_rows(value)):
                        taps_in[tap, to, :, lanes_of(tile)] = rows.astype(BF16)
                return carry

            lax.fori_loop(0, 16, one, 0)
            close_gap(taps_in, 8, tiles)

        def inner_inputs(tiles):
            columns = []
            for tap_x in range(3):
                for tap_y in range(3):
                    for tile in tiles:
                        columns.append(jnp.concatenate([
                            taps_in[tap_y, pl.ds(tap_x, 7), :, lanes_of(tile)].reshape(112, 128),
                            taps_in[tap_y, pl.ds(9 + tap_x, 7), :, lanes_of(tile)].reshape(112, 128),
                        ], axis=0))
            return jnp.concatenate(columns, axis=1)

        def silu(total, tile):
            value = total + bias
            value = value / (1.0 + jnp.exp(-value))
            if tile == 0:
                value = value * jnp.where(lane128 < 64, on_z, 1.0)
            if tile == 4:
                value = value * jnp.where(lane128 >= 64, on_z, 1.0)
            return value

        input_slots((0, 1, 2, 3), None)
        total = jnp.dot(
            inner_inputs((0, 1)), w1[0, :, pl.ds(128, 256), :].reshape(2304, 256), preferred_element_type=F32
        )
        partial[0] = total[:, :128]
        partial[1] = total[:, 128:]
        total = jnp.dot(inner_inputs((1, 2, 3)), w1[flag_z].reshape(3456, 256), preferred_element_type=F32)
        partial[2] = total[:, :128]
        partial[3] = total[:, 128:]
        partial[4] = jnp.dot(
            inner_inputs((3,)), w1c[:, pl.ds(0, 128), :].reshape(1152, 128), preferred_element_type=F32
        )

        for copy in copies(step, (0,)):
            copy.wait_recv()
        input_slots((4, 5), on_z)

        for place, row in enumerate((22, 23, 0, 1, 14, 15, 16, 17)):
            keep_row = on_y if row >= 16 else None
            for tile in range(TILES):
                value = flat[tile, pl.ds(2 * YS + row, 16, stride=YS), :]
                if keep_row is not None:
                    value = value * keep_row
                if tile >= 4:
                    value = value * on_z
                back = jnp.where(cut_back, 0.0, pltpu.roll(value, 1, 0))
                ahead = jnp.where(cut_ahead, 0.0, pltpu.roll(value, 15, 0))
                for tap, rows in enumerate((back, value, ahead)):
                    edge_in[tap, place, :, lanes_of(tile)] = rows.astype(BF16)

        def edge_inputs(tiles):
            columns = []
            for tap_x in range(3):
                for tap_y in range(3):
                    for tile in tiles:
                        columns.append(jnp.concatenate([
                            edge_in[tap_x, pl.ds(tap_y, 2), :, lanes_of(tile)].reshape(32, 128),
                            edge_in[tap_x, pl.ds(4 + tap_y, 2), :, lanes_of(tile)].reshape(32, 128),
                        ], axis=0))
            return jnp.concatenate(columns, axis=1)

        def keep_inner(total, tile):
            value = silu(total, tile)
            for x in range(1, 15):
                hidden[tile, x + 1, own_rows] = value[16 * x - 16 : 16 * x]

        def keep_edges(total, tile):
            value = silu(total, tile)
            for i, row in enumerate((23, 0, 15, 16)):
                flat_hidden[tile, pl.ds(YS + row, 16, stride=YS), :] = value[16 * i : 16 * i + 16]

        total = jnp.dot(
            inner_inputs((5,)), w1[0, :, pl.ds(0, 128), :].reshape(1152, 256), preferred_element_type=F32
        )
        keep_inner(partial[0] + total[:, :128], 0)
        keep_inner(partial[1] + total[:, 128:], 1)
        keep_inner(partial[2], 2)
        keep_inner(partial[3], 3)
        total = jnp.dot(
            inner_inputs((4,)), w1c[:, pl.ds(128, 128), :].reshape(1152, 128), preferred_element_type=F32
        )
        keep_inner(partial[4] + total, 4)
        total = jnp.dot(edge_inputs((5, 0, 1)), w1[0].reshape(3456, 256), preferred_element_type=F32)
        keep_edges(total[:, :128], 0)
        keep_edges(total[:, 128:], 1)
        total = jnp.dot(edge_inputs((1, 2, 3)), w1[flag_z].reshape(3456, 256), preferred_element_type=F32)
        keep_edges(total[:, :128], 2)
        keep_edges(total[:, 128:], 3)
        total = jnp.dot(edge_inputs((3, 4)), w1c[...].reshape(2304, 128), preferred_element_type=F32)
        keep_edges(total, 4)

        low = jnp.where(lane128 < 64, 1.0, 1.0 - on_z)
        high = jnp.where(lane128 >= 64, 1.0, 1.0 - on_z)

        def hidden_slot(slot, to, keep_x):
            sources = ((0, None), (1, None), (2, low), (2, high), (3, None), (4, None))
            for place, (tile, keep) in enumerate(sources):
                value = hidden[tile, slot]
                if keep is not None:
                    value = value * keep
                if keep_x is not None:
                    value = value * keep_x
                for tap, rows in enumerate(three_rows(value)):
                    taps_hid[tap, to, :, lanes_of(place)] = rows.astype(BF16)

        def inner_slot(slot, carry):
            hidden_slot(slot, slot + 2 * (slot >= 9).astype(jnp.int32), None)
            return carry

        lax.fori_loop(2, 16, inner_slot, 0)
        close_gap(taps_hid, 9, tuple(range(6)))

        def noise_of(half, low_slot, high_slot, slots):
            lanes = pl.ds(384 * half, 384)
            columns = []
            for tap_x in range(3):
                for tap_y in range(3):
                    columns.append(jnp.concatenate([
                        taps_hid[tap_y, pl.ds(start + tap_x, slots), :, lanes].reshape(16 * slots, 384)
                        for start in (low_slot, high_slot)
                    ], axis=0))
            values = jnp.concatenate(columns, axis=1)
            return jnp.dot(values, w2[...].reshape(3456, 256), preferred_element_type=F32)

        def update(noise, half, starts, slots):
            for part in range(2):
                tile = 2 * half + part
                for i, x in enumerate(starts):
                    place = pl.ds(2 + x, slots)
                    change = noise[16 * slots * i : 16 * slots * (i + 1), 128 * part : 128 * part + 128]
                    before = ext[step, tile, place, own_rows]
                    ext[step + 1, tile, place, own_rows] = before + delta * change.reshape(slots, 16, 128)

        for half in range(2):
            update(noise_of(half, 2, 10, 6), half, (2, 8), 6)

        def side_slot(x, to, keep):
            for tile in range(TILES):
                value = ext[step, tile, x + 2]
                if tile >= 4:
                    value = value * on_z
                if keep is not None:
                    value = value * keep
                for tap, rows in enumerate(three_rows(value)):
                    taps_side[tap, to, :, lanes_of(tile)] = rows.astype(BF16)

        for to, x in ((2, 0), (3, 1), (4, 14), (5, 15)):
            side_slot(x, to, None)
        for copy in copies(step, (-1, 1)):
            copy.wait_recv()
        for to, x in ((0, -2), (1, -1), (6, 16), (7, 17)):
            side_slot(x, to, on_x)

        keep_low = jnp.where(row8 < 2, on_x, 1.0)
        keep_high = jnp.where(row8 >= 6, on_x, 1.0)
        for tap_y in range(3):
            for tile in range(TILES):
                scale = on_z if tile >= 4 else 1.0
                for i, row in enumerate(((22 + tap_y) % 24, 15 + tap_y)):
                    first = flat[tile, pl.ds(row, 8, stride=YS), :] * (keep_low * scale)
                    last = flat[tile, pl.ds(12 * YS + row, 8, stride=YS), :] * (keep_high * scale)
                    for tap_x in range(3):
                        pair = [pltpu.roll(part, 8 - tap_x, 0) if tap_x else part for part in (first, last)]
                        rows = jnp.concatenate(pair, axis=0).astype(BF16)
                        edge_side[3 * tap_x + tap_y, pl.ds(16 * i, 16), lanes_of(tile)] = rows

        def side_inputs(tiles):
            columns = []
            for tap_x in range(3):
                for tap_y in range(3):
                    for tile in tiles:
                        columns.append(jnp.concatenate([
                            taps_side[tap_y, pl.ds(tap_x, 2), :, lanes_of(tile)].reshape(32, 128),
                            taps_side[tap_y, pl.ds(4 + tap_x, 2), :, lanes_of(tile)].reshape(32, 128),
                            edge_side[3 * tap_x + tap_y, :, lanes_of(tile)],
                        ], axis=0))
            return jnp.concatenate(columns, axis=1)

        def keep_side(total, tile):
            value = silu(total, tile)
            for i, slot in enumerate((0, 1, 16, 17)):
                hidden[tile, slot, own_rows] = value[16 * i : 16 * i + 16]
            for i, row in enumerate((23, 16)):
                for at, slot in ((0, 0), (1, 1), (12, 16), (13, 17)):
                    place = 64 + 16 * i + at
                    hidden[tile, slot, pl.ds(row, 1)] = value[place : place + 1]

        total = jnp.dot(side_inputs((5, 0, 1)), w1[0].reshape(3456, 256), preferred_element_type=F32)
        keep_side(total[:, :128], 0)
        keep_side(total[:, 128:], 1)
        total = jnp.dot(side_inputs((1, 2, 3)), w1[flag_z].reshape(3456, 256), preferred_element_type=F32)
        keep_side(total[:, :128], 2)
        keep_side(total[:, 128:], 3)
        total = jnp.dot(side_inputs((3, 4)), w1c[...].reshape(2304, 128), preferred_element_type=F32)
        keep_side(total, 4)
        hidden_slot(0, 0, on_x)
        hidden_slot(1, 1, None)
        hidden_slot(16, 18, None)
        hidden_slot(17, 19, on_x)
        for half in range(2):
            update(noise_of(half, 0, 16, 2), half, (0, 14), 2)

        @pl.when(step + 1 < steps)
        def _():
            for copy in copies(step + 1):
                copy.start()

        return carry

    lax.fori_loop(0, steps, step_body, 0)

    stores = [
        pltpu.make_async_copy(
            ext.at[steps, tile, pl.ds(2, 16), pl.ds(0, 16)],
            out_ref.at[:, :, pl.ds(128 * tile, 128)],
            load_sem.at[tile],
        )
        for tile in range(4)
    ]
    for store in stores:
        store.start()

    def drain(step, carry):
        for copy in copies(step):
            copy.wait_send()
        return carry

    lax.fori_loop(0, steps, drain, 0)
    for store in stores:
        store.wait()


def time_bias(timesteps, time_weight):
    half_c = time_weight.shape[0] // 2
    freqs = jnp.exp(-math.log(10000.0) * jnp.arange(half_c, dtype=F32) / half_c)
    angles = timesteps.astype(F32)[:, None] * freqs
    emb = jnp.concatenate([jnp.sin(angles), jnp.cos(angles)], axis=1)
    return jnp.dot(emb, time_weight, precision=lax.Precision.HIGHEST)


def shards(latent, conv_first, conv_second, time_weight, timesteps, offsets):
    steps = timesteps.shape[0]
    bias = time_bias(timesteps, time_weight)
    bias = jnp.concatenate([bias, bias], axis=1).reshape(steps, 1, 128)
    later = jnp.concatenate([timesteps[1:], jnp.zeros((1,), jnp.int32)])
    delta = (later - timesteps).astype(F32) / 1000.0
    vmem = pl.BlockSpec(memory_space=pltpu.VMEM)
    smem = pl.BlockSpec(memory_space=pltpu.SMEM)
    anywhere = pl.BlockSpec(memory_space=pl.ANY)
    count = len(DIRECTIONS)

    def body(*refs):
        kernel(steps, *refs)

    return pl.pallas_call(
        body,
        out_shape=jax.ShapeDtypeStruct(latent.shape, latent.dtype),
        in_specs=[anywhere, vmem, vmem, vmem, smem, smem],
        out_specs=anywhere,
        scratch_shapes=[
            pltpu.VMEM((steps + 1, TILES, XS, YS, 128), F32),
            pltpu.VMEM((2, 9, 384, 256), BF16),
            pltpu.VMEM((9, 256, 128), BF16),
            pltpu.VMEM((9, 384, 256), BF16),
            pltpu.VMEM((3, 18, 16, 768), BF16),
            pltpu.VMEM((3, 8, 16, 768), BF16),
            pltpu.VMEM((3, 8, 16, 768), BF16),
            pltpu.VMEM((9, 32, 768), BF16),
            pltpu.VMEM((5, 224, 128), F32),
            pltpu.VMEM((5, 18, YS, 128), F32),
            pltpu.VMEM((3, 20, 16, 768), BF16),
            pltpu.SemaphoreType.DMA((steps, count)),
            pltpu.SemaphoreType.DMA((steps, count)),
            pltpu.SemaphoreType.DMA((4,)),
        ],
        compiler_params=pltpu.CompilerParams(
            collective_id=0, has_side_effects=True, vmem_limit_bytes=48 * 2**20
        ),
    )(latent, conv_first.reshape(9, 192, 64), conv_second.reshape(9, 192, 64), bias, delta, offsets)


def solution(mesh):
    return jax.shard_map(
        shards,
        mesh=mesh,
        in_specs=(P("gx", "gy", "gz"), P(), P(), P(), P(), P()),
        out_specs=P("gx", "gy", "gz"),
        check_vma=False,
    )
```

time: 68.3 us -> 58.3 us (0.85)
  Pallas kernels: 63.7 us -> 53.4 us
    pallas_call x1, Pallas kernels: 63.7 us -> 53.4 us  [shards(): pl.pallas_call(body, out_shape=jax.ShapeDtypeStruct(latent.shape, latent....]
where the time goes in v1:
time: 58.3 us; the launch traced here: 57.9 us
  Pallas kernels  53.4 us (92%)
  local copies, waits for them, and re-layouts  3.18 us (5%)
  other arithmetic  1.01 us (2%)
    pallas_call x1, Pallas kernels, shards(): pl.pallas_call(body, out_shape=jax.ShapeDtypeStruct(latent.shape, latent....  53.4 us
    unnamed x13, local copies, waits for them, and re-layouts  3.11 us

profile of v1, /device:TPU:1, one launch (start us, length us, event | category | flops | bytes accessed | tf_op | source)
XLA Modules:
  0.0 57.9 jit_solution(13624739872361348110)
XLA Ops:
  0.0 0.0 copy-start
  0.0 0.0 copy-start.4
  0.0 0.7 %convert_element_type.6 = f32[4]{0:T(128)S(1)} convert(s32[4]{0:T(128)} %param.10) | non-fusion elementwise | flops 4 | bytes 32 | tf_op jit(solution)/shard_map/convert_element_type | solution.py:394
  0.7 0.0 copy-done.4
  0.7 0.1 slice.3
  0.8 0.1 fusion.5.refs_4_
  0.9 0.1 multiply_sine_fusion
  1.0 0.0 copy-done
  1.0 0.2 fusion
  1.2 0.1 pad_maximum_fusion
  1.3 0.0 copy-start.3
  1.3 1.3 %copy.7 = bf16[3,3,192,64]{3,2,1,0:T(8,128)(2,1)S(1)} copy(bf16[3,3,192,64]{2,3,1,0:T(8,128)(2,1)} %param.7) | data formatting | bytes 442368 | tf_op args[1]
  2.6 0.0 copy-start.1
  2.6 0.0 copy-done.3
  2.6 0.0 copy-start.2
  2.6 0.3 copy.8
  2.9 0.8 %copy-done.1 = f32[16,16,512]{2,1,0:T(8,128)S(1)} copy-done((f32[16,16,512]{2,1,0:T(8,128)S(1)}, f32[16,16,512]{2,1,0:T(8,128)}, u32[]{:S(2)}) %copy-start.1) | copy-done | bytes 524312
  3.6 0.0 copy-done.2
  3.6 53.4 %shard_map.64 = f32[16,16,512]{2,1,0:T(8,128)S(1)} custom-call(f32[16,16,512]{2,1,0:T(8,128)S(1)} %copy-done.1, bf16[9,192,64]{2,1,0:T(8,128)(2,1)S(1)} %bitcast.4, bf16[9,192,64]{2,1,0:T(8,128)(2,1)S(1)} %bitcast.5, f32[4,1,128]{2,1,0:T(1,128)S(1)} %bitcast.6, f32[4]{0:T(128)S(1)} %fusion.5.refs_4_, s32[4,3]{1,0:T(4,128)S(1)} %copy-done.2), custom_call_target="tpu_custom_call" | custom-call | tf_op jit(solution)/shard_map/pallas_call | solution.py:413
  57.1 0.8 %copy.10 = f32[16,16,512]{2,1,0:T(8,128)} copy(f32[16,16,512]{2,1,0:T(8,128)S(1)} %shard_map.64) | data formatting | bytes 1048576
  (1 shorter events, 0.0 us)
Async XLA Ops:
  0.0 1.0 %copy-start = (f32[64,64]{1,0:T(8,128)S(1)}, f32[64,64]{1,0:T(8,128)}, u32[]{:S(2)}) copy-start(f32[64,64]{1,0:T(8,128)} %param.9) | copy-start | bytes 49156
  0.0 0.7 %copy-start.4 = (s32[4]{0:T(128)S(1)}, s32[4]{0:T(128)}, u32[]{:S(2)}) copy-start(s32[4]{0:T(128)} %param.10) | copy-start | bytes 52
  1.3 1.3 %copy-start.3 = (bf16[3,3,192,64]{2,3,1,0:T(8,128)(2,1)S(1)}, bf16[3,3,192,64]{2,3,1,0:T(8,128)(2,1)}, u32[]{:S(2)}) copy-start(bf16[3,3,192,64]{2,3,1,0:T(8,128)(2,1)} %param.8) | copy-start | bytes 663556
  2.6 1.1 %copy-start.1 = (f32[16,16,512]{2,1,0:T(8,128)S(1)}, f32[16,16,512]{2,1,0:T(8,128)}, u32[]{:S(2)}) copy-start(f32[16,16,512]{2,1,0:T(8,128)} %refs_0_.1) | copy-start | bytes 1572868
  2.6 1.0 %copy-start.2 = (s32[4,3]{1,0:T(4,128)S(1)}, s32[4,3]{1,0:T(4,128)}, u32[]{:S(2)}) copy-start(s32[4,3]{1,0:T(4,128)} %refs_5_.1) | copy-start | bytes 148

commit v2 on v1

--- a/solution.py
+++ b/solution.py
@@ -23,15 +23,22 @@
 DIRECTIONS = directions()
 
 
-def sent(d):
-    x = {-1: pl.ds(2, 2), 0: pl.ds(2, 16), 1: pl.ds(16, 2)}[d[0]]
+WHOLE, INNER, SIDES = pl.ds(0, 16), pl.ds(0, 12), pl.ds(12, 4)
+
+
+def slot_of(x):
+    return (x - 2) % 16 if 0 <= x < 16 else x if x >= 16 else x + 20
+
+
+def sent(d, part):
+    x = {-1: pl.ds(14, 2), 0: part, 1: pl.ds(12, 2)}[d[0]]
     y = {-1: pl.ds(0, 2), 0: pl.ds(0, 16), 1: pl.ds(14, 2)}[d[1]]
     z = {-1: pl.ds(0, 1), 0: pl.ds(0, 4), 1: pl.ds(3, 1)}[d[2]]
     return z, x, y
 
 
-def landed(d):
-    x = {-1: pl.ds(18, 2), 0: pl.ds(2, 16), 1: pl.ds(0, 2)}[d[0]]
+def landed(d, part):
+    x = {-1: pl.ds(16, 2), 0: part, 1: pl.ds(18, 2)}[d[0]]
     y = {-1: pl.ds(16, 2), 0: pl.ds(0, 16), 1: pl.ds(22, 2)}[d[1]]
     z = {-1: pl.ds(4, 1), 0: pl.ds(0, 4), 1: pl.ds(5, 1)}[d[2]]
     return z, x, y
@@ -51,11 +58,12 @@
 ):
     loads = [
         pltpu.make_async_copy(
-            latent_ref.at[:, :, pl.ds(128 * tile, 128)],
-            ext.at[0, tile, pl.ds(2, 16), pl.ds(0, 16)],
-            load_sem.at[tile],
+            latent_ref.at[pl.ds(x, count), :, pl.ds(128 * tile, 128)],
+            ext.at[0, tile, pl.ds(slot_of(x), count), pl.ds(0, 16)],
+            load_sem.at[tile, i],
         )
         for tile in range(4)
+        for i, (x, count) in enumerate(((2, 14), (0, 2)))
     ]
     for load in loads:
         load.start()
@@ -66,18 +74,18 @@
     for load in loads:
         load.wait()
 
-    def copies(step, sides=(-1, 0, 1)):
+    def copies(step, sides=(-1, 0, 1), part=WHOLE, heights=(-1, 0, 1)):
         return [
             pltpu.make_async_remote_copy(
-                src_ref=ext.at[(step, *sent(d))],
-                dst_ref=ext.at[(step, *landed(d))],
+                src_ref=ext.at[(step, *sent(d, part))],
+                dst_ref=ext.at[(step, *landed(d, part))],
                 send_sem=send_sem.at[step, i],
                 recv_sem=recv_sem.at[step, i],
                 device_id=neighbour(d),
                 device_id_type=MESH,
             )
             for i, d in enumerate(DIRECTIONS)
-            if d[0] in sides
+            if d[0] in sides and d[2] in heights
         ]
 
     for copy in copies(0):
@@ -120,8 +128,8 @@
         off_x = 1.0 - on_x
         cut_down = row16 == 8 * flag_y
         cut_up = row16 == 15 - 8 * flag_y
-        cut_back = jnp.logical_and(row16 == 8, flag_x == 1)
-        cut_ahead = jnp.logical_and(row16 == 7, flag_x == 1)
+        cut_back = jnp.logical_and(row16 == 6, flag_x == 1)
+        cut_ahead = jnp.logical_and(row16 == 5, flag_x == 1)
         bias = bias_ref[step]
         delta = delta_ref[step]
         flat = ext.at[step].reshape(TILES, XS * YS, 128)
@@ -146,7 +154,7 @@
             def one(x, carry):
                 to = x + 2 * (x >= 8).astype(jnp.int32)
                 for tile in tiles:
-                    value = ext[step, tile, x + 2, own_rows]
+                    value = ext[step, tile, lax.rem(x + 14, 16), own_rows]
                     if keep is not None:
                         value = value * keep
                     for tap, rows in enumerate(three_rows(value)):
@@ -196,7 +204,7 @@
         for place, row in enumerate((22, 23, 0, 1, 14, 15, 16, 17)):
             keep_row = on_y if row >= 16 else None
             for tile in range(TILES):
-                value = flat[tile, pl.ds(2 * YS + row, 16, stride=YS), :]
+                value = flat[tile, pl.ds(row, 16, stride=YS), :]
                 if keep_row is not None:
                     value = value * keep_row
                 if tile >= 4:
@@ -220,12 +228,12 @@
         def keep_inner(total, tile):
             value = silu(total, tile)
             for x in range(1, 15):
-                hidden[tile, x + 1, own_rows] = value[16 * x - 16 : 16 * x]
+                hidden[tile, slot_of(x), own_rows] = value[16 * x - 16 : 16 * x]
 
         def keep_edges(total, tile):
             value = silu(total, tile)
             for i, row in enumerate((23, 0, 15, 16)):
-                flat_hidden[tile, pl.ds(YS + row, 16, stride=YS), :] = value[16 * i : 16 * i + 16]
+                flat_hidden[tile, pl.ds(row, 16, stride=YS), :] = value[16 * i : 16 * i + 16]
 
         total = jnp.dot(
             inner_inputs((5,)), w1[0, :, pl.ds(0, 128), :].reshape(1152, 256), preferred_element_type=F32
@@ -261,11 +269,11 @@
                 for tap, rows in enumerate(three_rows(value)):
                     taps_hid[tap, to, :, lanes_of(place)] = rows.astype(BF16)
 
-        def inner_slot(slot, carry):
-            hidden_slot(slot, slot + 2 * (slot >= 9).astype(jnp.int32), None)
+        def inner_slot(x, carry):
+            hidden_slot(lax.rem(x + 14, 16), x + 1 + 2 * (x >= 8).astype(jnp.int32), None)
             return carry
 
-        lax.fori_loop(2, 16, inner_slot, 0)
+        lax.fori_loop(1, 15, inner_slot, 0)
         close_gap(taps_hid, 9, tuple(range(6)))
 
         def noise_of(half, low_slot, high_slot, slots):
@@ -284,7 +292,7 @@
             for part in range(2):
                 tile = 2 * half + part
                 for i, x in enumerate(starts):
-                    place = pl.ds(2 + x, slots)
+                    place = pl.ds(slot_of(x), slots)
                     change = noise[16 * slots * i : 16 * slots * (i + 1), 128 * part : 128 * part + 128]
                     before = ext[step, tile, place, own_rows]
                     ext[step + 1, tile, place, own_rows] = before + delta * change.reshape(slots, 16, 128)
@@ -292,9 +300,14 @@
         for half in range(2):
             update(noise_of(half, 2, 10, 6), half, (2, 8), 6)
 
+        @pl.when(step + 1 < steps)
+        def _():
+            for copy in copies(step + 1, (0,), INNER):
+                copy.start()
+
         def side_slot(x, to, keep):
             for tile in range(TILES):
-                value = ext[step, tile, x + 2]
+                value = ext[step, tile, slot_of(x)]
                 if tile >= 4:
                     value = value * on_z
                 if keep is not None:
@@ -309,14 +322,14 @@
         for to, x in ((0, -2), (1, -1), (6, 16), (7, 17)):
             side_slot(x, to, on_x)
 
-        keep_low = jnp.where(row8 < 2, on_x, 1.0)
-        keep_high = jnp.where(row8 >= 6, on_x, 1.0)
+        keep_sides = jnp.where(row8 >= 4, on_x, 1.0)
         for tap_y in range(3):
             for tile in range(TILES):
                 scale = on_z if tile >= 4 else 1.0
                 for i, row in enumerate(((22 + tap_y) % 24, 15 + tap_y)):
-                    first = flat[tile, pl.ds(row, 8, stride=YS), :] * (keep_low * scale)
-                    last = flat[tile, pl.ds(12 * YS + row, 8, stride=YS), :] * (keep_high * scale)
+                    value = flat[tile, pl.ds(12 * YS + row, 8, stride=YS), :] * (keep_sides * scale)
+                    first = jnp.where(row8 < 2, pltpu.roll(value, 2, 0), value)
+                    last = jnp.where(row8 < 2, value, pltpu.roll(value, 6, 0))
                     for tap_x in range(3):
                         pair = [pltpu.roll(part, 8 - tap_x, 0) if tap_x else part for part in (first, last)]
                         rows = jnp.concatenate(pair, axis=0).astype(BF16)
@@ -336,10 +349,10 @@
 
         def keep_side(total, tile):
             value = silu(total, tile)
-            for i, slot in enumerate((0, 1, 16, 17)):
+            for i, slot in enumerate((17, 14, 13, 16)):
                 hidden[tile, slot, own_rows] = value[16 * i : 16 * i + 16]
             for i, row in enumerate((23, 16)):
-                for at, slot in ((0, 0), (1, 1), (12, 16), (13, 17)):
+                for at, slot in ((0, 17), (1, 14), (8, 13), (9, 16)):
                     place = 64 + 16 * i + at
                     hidden[tile, slot, pl.ds(row, 1)] = value[place : place + 1]
 
@@ -351,17 +364,18 @@
         keep_side(total[:, 128:], 3)
         total = jnp.dot(side_inputs((3, 4)), w1c[...].reshape(2304, 128), preferred_element_type=F32)
         keep_side(total, 4)
-        hidden_slot(0, 0, on_x)
-        hidden_slot(1, 1, None)
-        hidden_slot(16, 18, None)
-        hidden_slot(17, 19, on_x)
+        hidden_slot(17, 0, on_x)
+        hidden_slot(14, 1, None)
+        hidden_slot(13, 18, None)
+        hidden_slot(16, 19, on_x)
         for half in range(2):
             update(noise_of(half, 0, 16, 2), half, (0, 14), 2)
 
-        @pl.when(step + 1 < steps)
-        def _():
-            for copy in copies(step + 1):
-                copy.start()
+            @pl.when(step + 1 < steps)
+            def _():
+                if half:
+                    for copy in copies(step + 1, (0,), SIDES) + copies(step + 1, (-1, 1)):
+                        copy.start()
 
         return carry
 
@@ -369,11 +383,12 @@
 
     stores = [
         pltpu.make_async_copy(
-            ext.at[steps, tile, pl.ds(2, 16), pl.ds(0, 16)],
-            out_ref.at[:, :, pl.ds(128 * tile, 128)],
-            load_sem.at[tile],
+            ext.at[steps, tile, pl.ds(slot_of(x), count), pl.ds(0, 16)],
+            out_ref.at[pl.ds(x, count), :, pl.ds(128 * tile, 128)],
+            load_sem.at[tile, i],
         )
         for tile in range(4)
+        for i, (x, count) in enumerate(((2, 14), (0, 2)))
     ]
     for store in stores:
         store.start()
@@ -429,7 +444,7 @@
             pltpu.VMEM((3, 20, 16, 768), BF16),
             pltpu.SemaphoreType.DMA((steps, count)),
             pltpu.SemaphoreType.DMA((steps, count)),
-            pltpu.SemaphoreType.DMA((4,)),
+            pltpu.SemaphoreType.DMA((4, 2)),
         ],
         compiler_params=pltpu.CompilerParams(
             collective_id=0, has_side_effects=True, vmem_limit_bytes=48 * 2**20

time: 58.3 us -> 55.5 us (0.952)
  Pallas kernels: 53.4 us -> 50.9 us
    pallas_call x1, Pallas kernels: 53.4 us -> 50.9 us  [shards(): pl.pallas_call(body, out_shape=jax.ShapeDtypeStruct(latent.shape, latent....]
where the time goes in v2:
time: 55.5 us; the launch traced here: 55.3 us
  Pallas kernels  50.9 us (92%)
  local copies, waits for them, and re-layouts  3.18 us (6%)
  other arithmetic  1.01 us (2%)
    pallas_call x1, Pallas kernels, shards(): pl.pallas_call(body, out_shape=jax.ShapeDtypeStruct(latent.shape, latent....  50.9 us
    unnamed x13, local copies, waits for them, and re-layouts  3.11 us

profile of v2, /device:TPU:1, one launch (start us, length us, event | category | flops | bytes accessed | tf_op | source)
XLA Modules:
  0.0 55.3 jit_solution(9883251869472565181)
XLA Ops:
  0.0 0.0 copy-start
  0.0 0.0 copy-start.4
  0.0 0.7 %convert_element_type.6 = f32[4]{0:T(128)S(1)} convert(s32[4]{0:T(128)} %param.10) | non-fusion elementwise | flops 4 | bytes 32 | tf_op jit(solution)/shard_map/convert_element_type | solution.py:409
  0.7 0.0 copy-done.4
  0.7 0.1 slice.3
  0.8 0.1 fusion.5.refs_4_
  0.9 0.1 multiply_sine_fusion
  1.0 0.0 copy-done
  1.0 0.2 fusion
  1.2 0.1 pad_maximum_fusion
  1.3 0.0 copy-start.3
  1.3 1.3 %copy.7 = bf16[3,3,192,64]{3,2,1,0:T(8,128)(2,1)S(1)} copy(bf16[3,3,192,64]{2,3,1,0:T(8,128)(2,1)} %param.7) | data formatting | bytes 442368 | tf_op args[1]
  2.6 0.0 copy-start.1
  2.6 0.0 copy-done.3
  2.6 0.0 copy-start.2
  2.6 0.3 copy.8
  2.9 0.8 %copy-done.1 = f32[16,16,512]{2,1,0:T(8,128)S(1)} copy-done((f32[16,16,512]{2,1,0:T(8,128)S(1)}, f32[16,16,512]{2,1,0:T(8,128)}, u32[]{:S(2)}) %copy-start.1) | copy-done | bytes 524312
  3.6 0.0 copy-done.2
  3.6 50.9 %shard_map.64 = f32[16,16,512]{2,1,0:T(8,128)S(1)} custom-call(f32[16,16,512]{2,1,0:T(8,128)S(1)} %copy-done.1, bf16[9,192,64]{2,1,0:T(8,128)(2,1)S(1)} %bitcast.4, bf16[9,192,64]{2,1,0:T(8,128)(2,1)S(1)} %bitcast.5, f32[4,1,128]{2,1,0:T(1,128)S(1)} %bitcast.6, f32[4]{0:T(128)S(1)} %fusion.5.refs_4_, s32[4,3]{1,0:T(4,128)S(1)} %copy-done.2), custom_call_target="tpu_custom_call" | custom-call | tf_op jit(solution)/shard_map/pallas_call | solution.py:428
  54.5 0.8 %copy.10 = f32[16,16,512]{2,1,0:T(8,128)} copy(f32[16,16,512]{2,1,0:T(8,128)S(1)} %shard_map.64) | data formatting | bytes 1048576
  (1 shorter events, 0.0 us)
Async XLA Ops:
  0.0 1.0 %copy-start = (f32[64,64]{1,0:T(8,128)S(1)}, f32[64,64]{1,0:T(8,128)}, u32[]{:S(2)}) copy-start(f32[64,64]{1,0:T(8,128)} %param.9) | copy-start | bytes 49156
  0.0 0.7 %copy-start.4 = (s32[4]{0:T(128)S(1)}, s32[4]{0:T(128)}, u32[]{:S(2)}) copy-start(s32[4]{0:T(128)} %param.10) | copy-start | bytes 52
  1.3 1.3 %copy-start.3 = (bf16[3,3,192,64]{2,3,1,0:T(8,128)(2,1)S(1)}, bf16[3,3,192,64]{2,3,1,0:T(8,128)(2,1)}, u32[]{:S(2)}) copy-start(bf16[3,3,192,64]{2,3,1,0:T(8,128)(2,1)} %param.8) | copy-start | bytes 663556
  2.6 1.1 %copy-start.1 = (f32[16,16,512]{2,1,0:T(8,128)S(1)}, f32[16,16,512]{2,1,0:T(8,128)}, u32[]{:S(2)}) copy-start(f32[16,16,512]{2,1,0:T(8,128)} %refs_0_.1) | copy-start | bytes 1572868
  2.6 1.0 %copy-start.2 = (s32[4,3]{1,0:T(4,128)S(1)}, s32[4,3]{1,0:T(4,128)}, u32[]{:S(2)}) copy-start(s32[4,3]{1,0:T(4,128)} %refs_5_.1) | copy-start | bytes 148

commit v3 on v2

--- a/solution.py
+++ b/solution.py
@@ -53,9 +53,12 @@
 
 
 def kernel(
-    steps, latent_ref, first_ref, second_ref, bias_ref, delta_ref, offsets_ref, out_ref,
-    ext, w1, w1c, w2, taps_in, edge_in, taps_side, edge_side, partial, hidden, taps_hid, send_sem, recv_sem, load_sem,
+    steps, latent_ref, first_hbm, second_hbm, time_hbm, timesteps_hbm, offsets_hbm, out_ref,
+    first_ref, second_ref, time_ref, timesteps_ref, offsets_ref, ext, bias_ref, w1, w1c, w2, taps_in, edge_in, taps_side, edge_side, partial, hidden, taps_hid, send_sem, recv_sem, load_sem, small_sem,
 ):
+    barrier = pltpu.get_barrier_semaphore()
+    for d in DIRECTIONS:
+        pl.semaphore_signal(barrier, inc=1, device_id=neighbour(d), device_id_type=MESH)
     loads = [
         pltpu.make_async_copy(
             latent_ref.at[pl.ds(x, count), :, pl.ds(128 * tile, 128)],
@@ -65,11 +68,15 @@
         for tile in range(4)
         for i, (x, count) in enumerate(((2, 14), (0, 2)))
     ]
-    for load in loads:
+    small = [
+        pltpu.make_async_copy(source, target, small_sem.at[i])
+        for i, (source, target) in enumerate((
+            (first_hbm, first_ref), (second_hbm, second_ref), (time_hbm, time_ref),
+            (timesteps_hbm, timesteps_ref), (offsets_hbm, offsets_ref),
+        ))
+    ]
+    for load in loads + small:
         load.start()
-    barrier = pltpu.get_barrier_semaphore()
-    for d in DIRECTIONS:
-        pl.semaphore_signal(barrier, inc=1, device_id=neighbour(d), device_id_type=MESH)
     pl.semaphore_wait(barrier, len(DIRECTIONS))
     for load in loads:
         load.wait()
@@ -91,13 +98,15 @@
     for copy in copies(0):
         copy.start()
 
+    for load in small:
+        load.wait()
     w1[...] = jnp.zeros_like(w1)
     w1c[...] = jnp.zeros_like(w1c)
     w2[...] = jnp.zeros_like(w2)
 
     def place_weights(tap, carry):
-        one = first_ref[tap]
-        two = second_ref[tap]
+        one = first_ref[tap].T
+        two = second_ref[tap].T
         for out in range(4):
             rows = pl.ds(out * 64, 192)
             lanes = pl.ds(out * 64, 64)
@@ -112,6 +121,20 @@
         return carry
 
     lax.fori_loop(0, 9, place_weights, 0)
+
+    entry = lax.broadcasted_iota(jnp.int32, (64, 128), 0)
+    lane = lax.broadcasted_iota(jnp.int32, (64, 128), 1)
+    order = jnp.where(entry < 32, entry, entry - 32).astype(F32)
+    angles = jnp.zeros((64, 128), F32)
+    for step in range(steps):
+        angles = jnp.where(lane == step, timesteps_ref[step].astype(F32), angles)
+    angles = angles * jnp.exp(-math.log(10000.0) * order / 32)
+    embedding = jnp.where(entry < 32, jnp.sin(angles), jnp.cos(angles))
+    time_weight = time_ref[...]
+    for step in range(steps):
+        bias = jnp.sum(embedding[:, step : step + 1] * time_weight, axis=0, keepdims=True)
+        bias_ref[step, :, pl.ds(0, 64)] = bias
+        bias_ref[step, :, pl.ds(64, 64)] = bias
 
     row8 = lax.broadcasted_iota(jnp.int32, (8, 128), 0)
     row16 = lax.broadcasted_iota(jnp.int32, (16, 128), 0)
@@ -131,7 +154,8 @@
         cut_back = jnp.logical_and(row16 == 6, flag_x == 1)
         cut_ahead = jnp.logical_and(row16 == 5, flag_x == 1)
         bias = bias_ref[step]
-        delta = delta_ref[step]
+        later = jnp.where(step + 1 < steps, timesteps_ref[jnp.minimum(step + 1, steps - 1)], 0)
+        delta = jnp.full((1, 1, 128), (later - timesteps_ref[step]).astype(F32)) / 1000.0
         flat = ext.at[step].reshape(TILES, XS * YS, 128)
         flat_hidden = hidden.reshape(5, 18 * YS, 128)
 
@@ -403,22 +427,10 @@
         store.wait()
 
 
-def time_bias(timesteps, time_weight):
-    half_c = time_weight.shape[0] // 2
-    freqs = jnp.exp(-math.log(10000.0) * jnp.arange(half_c, dtype=F32) / half_c)
-    angles = timesteps.astype(F32)[:, None] * freqs
-    emb = jnp.concatenate([jnp.sin(angles), jnp.cos(angles)], axis=1)
-    return jnp.dot(emb, time_weight, precision=lax.Precision.HIGHEST)
-
-
 def shards(latent, conv_first, conv_second, time_weight, timesteps, offsets):
     steps = timesteps.shape[0]
-    bias = time_bias(timesteps, time_weight)
-    bias = jnp.concatenate([bias, bias], axis=1).reshape(steps, 1, 128)
-    later = jnp.concatenate([timesteps[1:], jnp.zeros((1,), jnp.int32)])
-    delta = (later - timesteps).astype(F32) / 1000.0
-    vmem = pl.BlockSpec(memory_space=pltpu.VMEM)
-    smem = pl.BlockSpec(memory_space=pltpu.SMEM)
+    first = jnp.swapaxes(conv_first, 2, 3).reshape(9, 64, 192)
+    second = jnp.swapaxes(conv_second, 2, 3).reshape(9, 64, 192)
     anywhere = pl.BlockSpec(memory_space=pl.ANY)
     count = len(DIRECTIONS)
 
@@ -428,10 +440,16 @@
     return pl.pallas_call(
         body,
         out_shape=jax.ShapeDtypeStruct(latent.shape, latent.dtype),
-        in_specs=[anywhere, vmem, vmem, vmem, smem, smem],
+        in_specs=[anywhere] * 6,
         out_specs=anywhere,
         scratch_shapes=[
+            pltpu.VMEM(first.shape, BF16),
+            pltpu.VMEM(second.shape, BF16),
+            pltpu.VMEM(time_weight.shape, F32),
+            pltpu.SMEM(timesteps.shape, jnp.int32),
+            pltpu.SMEM(offsets.shape, jnp.int32),
             pltpu.VMEM((steps + 1, TILES, XS, YS, 128), F32),
+            pltpu.VMEM((steps, 1, 128), F32),
             pltpu.VMEM((2, 9, 384, 256), BF16),
             pltpu.VMEM((9, 256, 128), BF16),
             pltpu.VMEM((9, 384, 256), BF16),
@@ -445,11 +463,12 @@
             pltpu.SemaphoreType.DMA((steps, count)),
             pltpu.SemaphoreType.DMA((steps, count)),
             pltpu.SemaphoreType.DMA((4, 2)),
+            pltpu.SemaphoreType.DMA((5,)),
         ],
         compiler_params=pltpu.CompilerParams(
-            collective_id=0, has_side_effects=True, vmem_limit_bytes=48 * 2**20
+            collective_id=0, has_side_effects=True, vmem_limit_bytes=60 * 2**20
         ),
-    )(latent, conv_first.reshape(9, 192, 64), conv_second.reshape(9, 192, 64), bias, delta, offsets)
+    )(latent, first, second, time_weight, timesteps, offsets)
 
 
 def solution(mesh):

time: 55.5 us -> 53 us (0.955)
  local copies, waits for them, and re-layouts: 3.18 us -> 1.88 us
  other arithmetic: 1.01 us -> 0 us
    unnamed x13 -> x1, local copies, waits for them, and re-layouts: 3.11 us -> 1.88 us
    convert_element_type x1 -> x0, other arithmetic: 0.73 us -> none  [time_bias(): angles = timesteps.astype(F32)[:, None] * freqs]
where the time goes in v3:
time: 53 us; the launch traced here: 52.8 us
  Pallas kernels  50.9 us (96%)
  local copies, waits for them, and re-layouts  1.88 us (4%)
    pallas_call x1, Pallas kernels, shards(): pl.pallas_call(body, out_shape=jax.ShapeDtypeStruct(latent.shape, latent....  50.9 us
    unnamed x1, local copies, waits for them, and re-layouts  1.88 us

profile of v3, /device:TPU:1, one launch (start us, length us, event | category | flops | bytes accessed | tf_op | source)
XLA Modules:
  0.0 52.8 jit_solution(17564495133685789015)
XLA Ops:
  0.0 50.9 %shard_map.64 = f32[16,16,512]{2,1,0:T(8,128)} custom-call(f32[16,16,512]{2,1,0:T(8,128)} %refs_0_.1, bf16[9,64,192]{2,1,0:T(8,128)(2,1)} %bitcast.6, bf16[9,64,192]{2,1,0:T(8,128)(2,1)} %bitcast.7, f32[64,64]{1,0:T(8,128)} %refs_3_.1, s32[4]{0:T(128)} %refs_4_.1, s32[4,3]{1,0:T(4,128)} %refs_5_.1), custom_call_target="tpu_custom_call" | custom-call | tf_op jit(solution)/shard_map/pallas_call | solution.py:440
  50.9 1.9 %copy.8 = f32[16,16,512]{2,1,0:T(8,128)} copy(f32[16,16,512]{2,1,0:T(8,128)} %shard_map.64) | data formatting | bytes 1048576

commit v4 on v3

--- a/solution.py
+++ b/solution.py
@@ -44,18 +44,23 @@
     return z, x, y
 
 
-def neighbour(d):
-    place = []
-    for name, by in zip(("gx", "gy", "gz"), d):
-        size = lax.axis_size(name)
-        place.append(lax.rem(lax.axis_index(name) + by + size, size))
-    return tuple(place)
+def surroundings():
+    places = []
+    for name in ("gx", "gy", "gz"):
+        size, me = lax.axis_size(name), lax.axis_index(name)
+        places.append((lax.rem(me + size - 1, size), me, lax.rem(me + 1, size)))
+    return places
 
 
 def kernel(
     steps, latent_ref, first_hbm, second_hbm, time_hbm, timesteps_hbm, offsets_hbm, out_ref,
-    first_ref, second_ref, time_ref, timesteps_ref, offsets_ref, ext, bias_ref, w1, w1c, w2, taps_in, edge_in, taps_side, edge_side, partial, hidden, taps_hid, send_sem, recv_sem, load_sem, small_sem,
+    first_ref, second_ref, time_ref, timesteps_ref, offsets_ref, ext, bias_ref, w1, w1c, w2, taps_in, edge_in, taps_side, edge_side, partial, side_partial, hidden, taps_hid, send_sem, recv_sem, load_sem, small_sem,
 ):
+    places = surroundings()
+
+    def neighbour(d):
+        return tuple(place[by + 1] for place, by in zip(places, d))
+
     barrier = pltpu.get_barrier_semaphore()
     for d in DIRECTIONS:
         pl.semaphore_signal(barrier, inc=1, device_id=neighbour(d), device_id_type=MESH)
@@ -176,16 +181,17 @@
 
         def input_slots(tiles, keep):
             def one(x, carry):
-                to = x + 2 * (x >= 8).astype(jnp.int32)
+                to = x + 2 * (x >= 8)
                 for tile in tiles:
-                    value = ext[step, tile, lax.rem(x + 14, 16), own_rows]
+                    value = ext[step, tile, slot_of(x), own_rows]
                     if keep is not None:
                         value = value * keep
                     for tap, rows in enumerate(three_rows(value)):
                         taps_in[tap, to, :, lanes_of(tile)] = rows.astype(BF16)
                 return carry
 
-            lax.fori_loop(0, 16, one, 0)
+            for x in range(16):
+                one(x, 0)
             close_gap(taps_in, 8, tiles)
 
         def inner_inputs(tiles):
@@ -221,22 +227,28 @@
             inner_inputs((3,)), w1c[:, pl.ds(0, 128), :].reshape(1152, 128), preferred_element_type=F32
         )
 
+        def outer_rows(places, tiles):
+            for place in places:
+                row = (22, 23, 0, 1, 14, 15, 16, 17)[place]
+                for tile in tiles:
+                    value = flat[tile, pl.ds(row, 16, stride=YS), :]
+                    if row >= 16:
+                        value = value * on_y
+                    if tile >= 4:
+                        value = value * on_z
+                    back = jnp.where(cut_back, 0.0, pltpu.roll(value, 1, 0))
+                    ahead = jnp.where(cut_ahead, 0.0, pltpu.roll(value, 15, 0))
+                    for tap, rows in enumerate((back, value, ahead)):
+                        edge_in[tap, place, :, lanes_of(tile)] = rows.astype(BF16)
+
+        outer_rows((2, 3, 4, 5), range(4))
+
         for copy in copies(step, (0,)):
             copy.wait_recv()
         input_slots((4, 5), on_z)
 
-        for place, row in enumerate((22, 23, 0, 1, 14, 15, 16, 17)):
-            keep_row = on_y if row >= 16 else None
-            for tile in range(TILES):
-                value = flat[tile, pl.ds(row, 16, stride=YS), :]
-                if keep_row is not None:
-                    value = value * keep_row
-                if tile >= 4:
-                    value = value * on_z
-                back = jnp.where(cut_back, 0.0, pltpu.roll(value, 1, 0))
-                ahead = jnp.where(cut_ahead, 0.0, pltpu.roll(value, 15, 0))
-                for tap, rows in enumerate((back, value, ahead)):
-                    edge_in[tap, place, :, lanes_of(tile)] = rows.astype(BF16)
+        outer_rows(range(8), (4, 5))
+        outer_rows((0, 1, 6, 7), range(4))
 
         def edge_inputs(tiles):
             columns = []
@@ -294,19 +306,19 @@
                     taps_hid[tap, to, :, lanes_of(place)] = rows.astype(BF16)
 
         def inner_slot(x, carry):
-            hidden_slot(lax.rem(x + 14, 16), x + 1 + 2 * (x >= 8).astype(jnp.int32), None)
-            return carry
-
-        lax.fori_loop(1, 15, inner_slot, 0)
+            hidden_slot(slot_of(x), x + 1 + 2 * (x >= 8), None)
+
+        for x in range(1, 15):
+            inner_slot(x, 0)
         close_gap(taps_hid, 9, tuple(range(6)))
 
-        def noise_of(half, low_slot, high_slot, slots):
-            lanes = pl.ds(384 * half, 384)
+        def noise_of(halves, low_slot, high_slot, slots):
             columns = []
             for tap_x in range(3):
                 for tap_y in range(3):
                     columns.append(jnp.concatenate([
-                        taps_hid[tap_y, pl.ds(start + tap_x, slots), :, lanes].reshape(16 * slots, 384)
+                        taps_hid[tap_y, pl.ds(start + tap_x, slots), :, pl.ds(384 * half, 384)].reshape(16 * slots, 384)
+                        for half in halves
                         for start in (low_slot, high_slot)
                     ], axis=0))
             values = jnp.concatenate(columns, axis=1)
@@ -322,15 +334,15 @@
                     ext[step + 1, tile, place, own_rows] = before + delta * change.reshape(slots, 16, 128)
 
         for half in range(2):
-            update(noise_of(half, 2, 10, 6), half, (2, 8), 6)
+            update(noise_of((half,), 2, 10, 6), half, (2, 8), 6)
 
         @pl.when(step + 1 < steps)
         def _():
             for copy in copies(step + 1, (0,), INNER):
                 copy.start()
 
-        def side_slot(x, to, keep):
-            for tile in range(TILES):
+        def side_slot(x, to, keep, tiles=tuple(range(TILES))):
+            for tile in tiles:
                 value = ext[step, tile, slot_of(x)]
                 if tile >= 4:
                     value = value * on_z
@@ -341,23 +353,30 @@
 
         for to, x in ((2, 0), (3, 1), (4, 14), (5, 15)):
             side_slot(x, to, None)
-        for copy in copies(step, (-1, 1)):
+        keep_sides = jnp.where(row8 >= 4, on_x, 1.0)
+
+        def side_edges(tile, taps):
+            scale = on_z if tile >= 4 else 1.0
+            for i, tap_y in taps:
+                row = (15 + tap_y) if i else (22 + tap_y) % 24
+                value = flat[tile, pl.ds(12 * YS + row, 8, stride=YS), :] * (keep_sides * scale)
+                first = jnp.where(row8 < 2, pltpu.roll(value, 2, 0), value)
+                last = jnp.where(row8 < 2, value, pltpu.roll(value, 6, 0))
+                for tap_x in range(3):
+                    pair = [pltpu.roll(part, 8 - tap_x, 0) if tap_x else part for part in (first, last)]
+                    rows = jnp.concatenate(pair, axis=0).astype(BF16)
+                    edge_side[3 * tap_x + tap_y, pl.ds(16 * i, 16), lanes_of(tile)] = rows
+
+        far_rows, near_rows = ((0, 0), (0, 1), (1, 1), (1, 2)), ((0, 2), (1, 0))
+        halo_slots = ((0, -2), (1, -1), (6, 16), (7, 17))
+        across = copies(step, (-1, 1))
+        others, faces = across[:-2], across[-2:]
+        for copy in others:
             copy.wait_recv()
-        for to, x in ((0, -2), (1, -1), (6, 16), (7, 17)):
-            side_slot(x, to, on_x)
-
-        keep_sides = jnp.where(row8 >= 4, on_x, 1.0)
-        for tap_y in range(3):
-            for tile in range(TILES):
-                scale = on_z if tile >= 4 else 1.0
-                for i, row in enumerate(((22 + tap_y) % 24, 15 + tap_y)):
-                    value = flat[tile, pl.ds(12 * YS + row, 8, stride=YS), :] * (keep_sides * scale)
-                    first = jnp.where(row8 < 2, pltpu.roll(value, 2, 0), value)
-                    last = jnp.where(row8 < 2, value, pltpu.roll(value, 6, 0))
-                    for tap_x in range(3):
-                        pair = [pltpu.roll(part, 8 - tap_x, 0) if tap_x else part for part in (first, last)]
-                        rows = jnp.concatenate(pair, axis=0).astype(BF16)
-                        edge_side[3 * tap_x + tap_y, pl.ds(16 * i, 16), lanes_of(tile)] = rows
+        for to, x in halo_slots:
+            side_slot(x, to, on_x, (4, 5))
+        for tile in range(TILES):
+            side_edges(tile, far_rows + near_rows if tile >= 4 else far_rows)
 
         def side_inputs(tiles):
             columns = []
@@ -380,20 +399,37 @@
                     place = 64 + 16 * i + at
                     hidden[tile, slot, pl.ds(row, 1)] = value[place : place + 1]
 
-        total = jnp.dot(side_inputs((5, 0, 1)), w1[0].reshape(3456, 256), preferred_element_type=F32)
+        side_partial[:, pl.ds(0, 256)] = jnp.dot(
+            side_inputs((5,)), w1[0, :, pl.ds(0, 128), :].reshape(1152, 256), preferred_element_type=F32
+        )
+        side_partial[:, pl.ds(256, 128)] = jnp.dot(
+            side_inputs((4,)), w1c[:, pl.ds(128, 128), :].reshape(1152, 128), preferred_element_type=F32
+        )
+        for copy in faces:
+            copy.wait_recv()
+        for to, x in halo_slots:
+            side_slot(x, to, on_x, (0, 1, 2, 3))
+        for tile in range(4):
+            side_edges(tile, near_rows)
+        total = side_partial[:, pl.ds(0, 256)] + jnp.dot(
+            side_inputs((0, 1)), w1[0, :, pl.ds(128, 256), :].reshape(2304, 256), preferred_element_type=F32
+        )
         keep_side(total[:, :128], 0)
         keep_side(total[:, 128:], 1)
         total = jnp.dot(side_inputs((1, 2, 3)), w1[flag_z].reshape(3456, 256), preferred_element_type=F32)
         keep_side(total[:, :128], 2)
         keep_side(total[:, 128:], 3)
-        total = jnp.dot(side_inputs((3, 4)), w1c[...].reshape(2304, 128), preferred_element_type=F32)
+        total = side_partial[:, pl.ds(256, 128)] + jnp.dot(
+            side_inputs((3,)), w1c[:, pl.ds(0, 128), :].reshape(1152, 128), preferred_element_type=F32
+        )
         keep_side(total, 4)
         hidden_slot(17, 0, on_x)
         hidden_slot(14, 1, None)
         hidden_slot(13, 18, None)
         hidden_slot(16, 19, on_x)
+        noise = noise_of((0, 1), 0, 16, 2)
         for half in range(2):
-            update(noise_of(half, 0, 16, 2), half, (0, 14), 2)
+            update(noise[64 * half : 64 * half + 64], half, (0, 14), 2)
 
             @pl.when(step + 1 < steps)
             def _():
@@ -458,6 +494,7 @@
             pltpu.VMEM((3, 8, 16, 768), BF16),
             pltpu.VMEM((9, 32, 768), BF16),
             pltpu.VMEM((5, 224, 128), F32),
+            pltpu.VMEM((96, 384), F32),
             pltpu.VMEM((5, 18, YS, 128), F32),
             pltpu.VMEM((3, 20, 16, 768), BF16),
             pltpu.SemaphoreType.DMA((steps, count)),

time: 53 us -> 51.4 us (0.970)
  Pallas kernels: 50.9 us -> 49.4 us
    pallas_call x1, Pallas kernels: 50.9 us -> 49.4 us  [shards(): pl.pallas_call(body, out_shape=jax.ShapeDtypeStruct(latent.shape, latent....]
where the time goes in v4:
time: 51.4 us; the launch traced here: 51.3 us
  Pallas kernels  49.4 us (96%)
  local copies, waits for them, and re-layouts  1.88 us (4%)
    pallas_call x1, Pallas kernels, shards(): pl.pallas_call(body, out_shape=jax.ShapeDtypeStruct(latent.shape, latent....  49.4 us
    unnamed x1, local copies, waits for them, and re-layouts  1.88 us

profile of v4, /device:TPU:1, one launch (start us, length us, event | category | flops | bytes accessed | tf_op | source)
XLA Modules:
  0.0 51.3 jit_solution(15409167910750115823)
XLA Ops:
  0.0 49.4 %shard_map.64 = f32[16,16,512]{2,1,0:T(8,128)} custom-call(f32[16,16,512]{2,1,0:T(8,128)} %refs_0_.1, bf16[9,64,192]{2,1,0:T(8,128)(2,1)} %bitcast.6, bf16[9,64,192]{2,1,0:T(8,128)(2,1)} %bitcast.7, f32[64,64]{1,0:T(8,128)} %refs_3_.1, s32[4]{0:T(128)} %refs_4_.1, s32[4,3]{1,0:T(4,128)} %refs_5_.1), custom_call_target="tpu_custom_call" | custom-call | tf_op jit(solution)/shard_map/pallas_call | solution.py:476
  49.4 1.9 %copy.8 = f32[16,16,512]{2,1,0:T(8,128)} copy(f32[16,16,512]{2,1,0:T(8,128)} %shard_map.64) | data formatting | bytes 1048576

commit v5 on v4

--- a/solution.py
+++ b/solution.py
@@ -145,6 +145,17 @@
     row16 = lax.broadcasted_iota(jnp.int32, (16, 128), 0)
     lane128 = lax.broadcasted_iota(jnp.int32, (1, 128), 1)
     own_rows = pl.ds(0, 16)
+
+    def stores(first, parts):
+        return [
+            pltpu.make_async_copy(
+                ext.at[steps, tile, pl.ds(slot_of(x), count), pl.ds(0, 16)],
+                out_ref.at[pl.ds(x, count), :, pl.ds(128 * tile, 128)],
+                load_sem.at[tile, first + i],
+            )
+            for tile in range(4)
+            for i, (x, count) in enumerate(parts)
+        ]
 
     def step_body(step, carry):
         flag_x = offsets_ref[step, 0]
@@ -312,14 +323,14 @@
             inner_slot(x, 0)
         close_gap(taps_hid, 9, tuple(range(6)))
 
-        def noise_of(halves, low_slot, high_slot, slots):
+        def noise_of(halves, starts, slots):
             columns = []
             for tap_x in range(3):
                 for tap_y in range(3):
                     columns.append(jnp.concatenate([
                         taps_hid[tap_y, pl.ds(start + tap_x, slots), :, pl.ds(384 * half, 384)].reshape(16 * slots, 384)
                         for half in halves
-                        for start in (low_slot, high_slot)
+                        for start in starts
                     ], axis=0))
             values = jnp.concatenate(columns, axis=1)
             return jnp.dot(values, w2[...].reshape(3456, 256), preferred_element_type=F32)
@@ -333,13 +344,20 @@
                     before = ext[step, tile, place, own_rows]
                     ext[step + 1, tile, place, own_rows] = before + delta * change.reshape(slots, 16, 128)
 
-        for half in range(2):
-            update(noise_of((half,), 2, 10, 6), half, (2, 8), 6)
+        for start, x in ((2, 2), (10, 8)):
+            noise = noise_of((0, 1), (start,), 6)
+            for half in range(2):
+                update(noise[96 * half : 96 * half + 96], half, (x,), 6)
 
         @pl.when(step + 1 < steps)
         def _():
             for copy in copies(step + 1, (0,), INNER):
                 copy.start()
+
+        @pl.when(step + 1 == steps)
+        def _():
+            for store in stores(2, ((2, 12),)):
+                store.start()
 
         def side_slot(x, to, keep, tiles=tuple(range(TILES))):
             for tile in tiles:
@@ -427,7 +445,7 @@
         hidden_slot(14, 1, None)
         hidden_slot(13, 18, None)
         hidden_slot(16, 19, on_x)
-        noise = noise_of((0, 1), 0, 16, 2)
+        noise = noise_of((0, 1), (0, 16), 2)
         for half in range(2):
             update(noise[64 * half : 64 * half + 64], half, (0, 14), 2)
 
@@ -441,16 +459,7 @@
 
     lax.fori_loop(0, steps, step_body, 0)
 
-    stores = [
-        pltpu.make_async_copy(
-            ext.at[steps, tile, pl.ds(slot_of(x), count), pl.ds(0, 16)],
-            out_ref.at[pl.ds(x, count), :, pl.ds(128 * tile, 128)],
-            load_sem.at[tile, i],
-        )
-        for tile in range(4)
-        for i, (x, count) in enumerate(((2, 14), (0, 2)))
-    ]
-    for store in stores:
+    for store in stores(0, ((0, 2), (14, 2))):
         store.start()
 
     def drain(step, carry):
@@ -459,7 +468,7 @@
         return carry
 
     lax.fori_loop(0, steps, drain, 0)
-    for store in stores:
+    for store in stores(0, ((0, 2), (14, 2))) + stores(2, ((2, 12),)):
         store.wait()
 
 
@@ -499,7 +508,7 @@
             pltpu.VMEM((3, 20, 16, 768), BF16),
             pltpu.SemaphoreType.DMA((steps, count)),
             pltpu.SemaphoreType.DMA((steps, count)),
-            pltpu.SemaphoreType.DMA((4, 2)),
+            pltpu.SemaphoreType.DMA((4, 3)),
             pltpu.SemaphoreType.DMA((5,)),
         ],
         compiler_params=pltpu.CompilerParams(

time: 51.4 us -> 51.3 us (level)
  no operation moved by 1% of the time
where the time goes in v5:
time: 51.3 us; the launch traced here: 51.1 us
  Pallas kernels  49.2 us (96%)
  local copies, waits for them, and re-layouts  1.88 us (4%)
    pallas_call x1, Pallas kernels, shards(): pl.pallas_call(body, out_shape=jax.ShapeDtypeStruct(latent.shape, latent....  49.2 us
    unnamed x1, local copies, waits for them, and re-layouts  1.88 us

profile of v5, /device:TPU:1, one launch (start us, length us, event | category | flops | bytes accessed | tf_op | source)
XLA Modules:
  0.0 51.1 jit_solution(13893896472704943710)
XLA Ops:
  0.0 49.2 %shard_map.64 = f32[16,16,512]{2,1,0:T(8,128)} custom-call(f32[16,16,512]{2,1,0:T(8,128)} %refs_0_.1, bf16[9,64,192]{2,1,0:T(8,128)(2,1)} %bitcast.6, bf16[9,64,192]{2,1,0:T(8,128)(2,1)} %bitcast.7, f32[64,64]{1,0:T(8,128)} %refs_3_.1, s32[4]{0:T(128)} %refs_4_.1, s32[4,3]{1,0:T(4,128)} %refs_5_.1), custom_call_target="tpu_custom_call" | custom-call | tf_op jit(solution)/shard_map/pallas_call | solution.py:485
  49.2 1.9 %copy.8 = f32[16,16,512]{2,1,0:T(8,128)} copy(f32[16,16,512]{2,1,0:T(8,128)} %shard_map.64) | data formatting | bytes 1048576

commit v6 on v5

--- a/solution.py
+++ b/solution.py
@@ -17,7 +17,7 @@
 
 def directions():
     every = [d for d in itertools.product((-1, 0, 1), repeat=3) if d != (0, 0, 0)]
-    return sorted(every, key=lambda d: (d[0] != 0, -sum(map(abs, d))))
+    return sorted(every, key=lambda d: (d[0] != 0, -sum(map(abs, d)), d[0] * d[1], d[0] * d[2]))
 
 
 DIRECTIONS = directions()

time: 51.3 us -> 51 us (level)
  no operation moved by 1% of the time
where the time goes in v6:
time: 51 us; the launch traced here: 50.9 us
  Pallas kernels  49 us (96%)
  local copies, waits for them, and re-layouts  1.88 us (4%)
    pallas_call x1, Pallas kernels, shards(): pl.pallas_call(body, out_shape=jax.ShapeDtypeStruct(latent.shape, latent....  49 us
    unnamed x1, local copies, waits for them, and re-layouts  1.88 us

profile of v6, /device:TPU:1, one launch (start us, length us, event | category | flops | bytes accessed | tf_op | source)
XLA Modules:
  0.0 50.9 jit_solution(11826318703570891674)
XLA Ops:
  0.0 49.0 %shard_map.64 = f32[16,16,512]{2,1,0:T(8,128)} custom-call(f32[16,16,512]{2,1,0:T(8,128)} %refs_0_.1, bf16[9,64,192]{2,1,0:T(8,128)(2,1)} %bitcast.6, bf16[9,64,192]{2,1,0:T(8,128)(2,1)} %bitcast.7, f32[64,64]{1,0:T(8,128)} %refs_3_.1, s32[4]{0:T(128)} %refs_4_.1, s32[4,3]{1,0:T(4,128)} %refs_5_.1), custom_call_target="tpu_custom_call" | custom-call | tf_op jit(solution)/shard_map/pallas_call | solution.py:485
  49.0 1.9 %copy.8 = f32[16,16,512]{2,1,0:T(8,128)} copy(f32[16,16,512]{2,1,0:T(8,128)} %shard_map.64) | data formatting | bytes 1048576
